TPU v7x, 32 devices: a whole 2x2x4 slice. The times are simulated.
32 devices in a mesh: rows: 16 (over z, x, core), heads: 2 (over y).
Axes of the slice: x: 2, y: 2, z: 4, core: 2. Of those that a mesh axis runs over, the one named last changes fastest.
Arguments:
- hidden: bfloat16 [2, 16, 8192], P(None, None, 'rows'), may hold values from -6 to 6
- norm_gain: bfloat16 [8192], P('rows'), may hold values from 0.5 to 2
- query_weight: bfloat16 [8192, 8192], P('rows', 'heads'), may hold values from -0.0625 to 0.0625
- query_gain: bfloat16 [128], replicated, may hold values from 0.5 to 2
- out_weight: bfloat16 [8192, 8192], P('heads', 'rows'), may hold values from -0.0625 to 0.0625
- attn_gate: float32 [1], replicated, may hold values from 0.3 to 1.5
- kv_cache: bfloat16 [16, 8, 4, 1408, 256], P('rows', 'heads'), may hold values from -384 to 384
- new_tiles: bfloat16 [16, 8, 1408, 256], P('rows', 'heads'), may hold values from -384 to 384
- counts: int32 [2, 16], P(None, 'rows'), may hold values from 1 to 4, as said below
- join_list: int32 [2, 2, 3], replicated, may hold values from 0 to 15, as said below
Outputs:
- mixed: bfloat16 [2, 16, 8192], P(None, None, 'rows')
- arrived: bfloat16 [16, 8, 1408, 256], P('rows', 'heads')
Inputs may be any that keep to these rules, and one draw needn't show every extreme that they name: Some row has 4 tiles and some row one tile at each step; a row that receives a tile in slot k at some step counts more than k tiles at that step and every later one. `join_list`: sources are distinct over all entries, below 16; targets are distinct over all entries, below 16; slots are below 4.
All inputs are finite; a program needn't handle non-finite values.
Results may differ from a plain program's by a relative error of at most 0.0045.
The roundings to bfloat16 on the way count: a program that leaves them out, or rounds other values in their place, can miss the bound.
Values may be sent and summed in bfloat16 or wider, within the bound.
No kernel may reach another device: no remote copies, remote signals or barrier semaphores. Data moves between devices by JAX's collectives and lax.ppermute only.
A program may use at most 128 MiB of HBM per device.

v0:
```python
import math

import jax
import jax.numpy as jnp
from jax import lax
from jax.sharding import PartitionSpec as P

STEPS = 2
JOINS = 2


epsilon = 1e-05


def broadcast(block, axis, owner):
    block = jnp.where(lax.axis_index(axis) == owner, block, jnp.zeros_like(block))
    return lax.psum(block, axis)


def place_tile(kv_state, new_block, local_row, slot_index):
    rows_here = kv_state.shape[0]
    anchor = jnp.int32(0)
    inside = (local_row >= 0) & (local_row < rows_here)
    row_index = jnp.clip(local_row, 0, rows_here - 1)
    sizes = (1, kv_state.shape[1], 1, kv_state.shape[3], kv_state.shape[4])
    previous = lax.dynamic_slice(kv_state, (row_index, anchor, slot_index, anchor, anchor), sizes)
    updated = jnp.where(inside, new_block[None, :, None], previous)
    return lax.dynamic_update_slice(
        kv_state, updated, (row_index, anchor, slot_index, anchor, anchor)
    )


def place_arrival(arrived_state, new_block, local_row):
    rows_here = arrived_state.shape[0]
    inside = (local_row >= 0) & (local_row < rows_here)
    updated = jnp.where(inside, new_block[None], arrived_state)
    return updated


def on_device(
    hidden,
    norm_gain,
    query_weight,
    query_gain,
    out_weight,
    attn_gate,
    kv_cache,
    new_tiles,
    counts,
    join_list,
):
    rows_here = kv_cache.shape[0]
    kv_here = kv_cache.shape[1]
    slot_count = kv_cache.shape[2]
    tile_len = kv_cache.shape[3]
    head_size = kv_cache.shape[4] // 2
    heads_here = query_weight.shape[1] // head_size
    group_size = heads_here // kv_here
    my_index = lax.axis_index("rows")
    first_row = my_index * rows_here
    gain_wide = norm_gain.astype(jnp.float32)
    own_tile = new_tiles[0]
    kv_state = kv_cache
    arrived_state = jnp.zeros((rows_here, kv_here, tile_len, 2 * head_size), jnp.bfloat16)
    positions = jnp.arange(slot_count * tile_len, dtype=jnp.int32)
    outputs = []
    for decode_step in range(STEPS):
        for join_index in range(JOINS):
            source = join_list[decode_step, join_index, 0]
            target = join_list[decode_step, join_index, 1]
            slot_index = join_list[decode_step, join_index, 2]
            new_block = broadcast(own_tile, "rows", source)
            kv_state = place_tile(kv_state, new_block, target - first_row, slot_index)
            arrived_state = place_arrival(arrived_state, new_block, target - first_row)
        tokens = hidden[decode_step]
        tokens_wide = tokens.astype(jnp.float32)
        scaled = (tokens_wide * gain_wide).astype(jnp.bfloat16)
        raw_query = lax.psum_scatter(
            jnp.dot(scaled, query_weight, preferred_element_type=jnp.float32),
            "rows",
            scatter_dimension=0,
            tiled=True,
        )
        queries = raw_query.reshape(rows_here, heads_here, head_size)
        queries = (
            queries
            * lax.rsqrt(jnp.mean(queries * queries, axis=-1, keepdims=True) + epsilon)
            * query_gain.astype(jnp.float32)
        )
        queries = queries.astype(jnp.bfloat16).reshape(rows_here, kv_here, group_size, head_size)
        flat_cache = kv_state.reshape(rows_here, kv_here, slot_count * tile_len, 2 * head_size)
        cached_keys = flat_cache[..., :head_size]
        cached_values = flat_cache[..., head_size:]
        scores = jnp.einsum(
            "rkgd,rktd->rkgt", queries, cached_keys, preferred_element_type=jnp.float32
        ) * (1.0 / math.sqrt(head_size))
        lengths = counts[decode_step] * tile_len
        usable = (positions[None, :] < lengths[:, None])[:, None, None, :]
        scores = jnp.where(usable, scores, -1e30)
        highest = jnp.max(scores, axis=-1, keepdims=True)
        exponent = jnp.where(usable, jnp.exp(scores - highest), 0.0)
        probs = (exponent / jnp.sum(exponent, axis=-1, keepdims=True)).astype(jnp.bfloat16)
        context = jnp.einsum(
            "rkgt,rktd->rkgd", probs, cached_values, preferred_element_type=jnp.float32
        )
        context = context.astype(jnp.bfloat16).reshape(rows_here, heads_here * head_size)
        partial_value = jnp.dot(
            lax.all_gather(context, "rows", axis=0, tiled=True),
            out_weight,
            preferred_element_type=jnp.float32,
        )
        projected = lax.psum(partial_value, "heads")
        outputs.append((tokens_wide + jnp.tanh(attn_gate[0]) * projected).astype(jnp.bfloat16))
    return (jnp.stack(outputs), arrived_state)


def solution(mesh):
    in_specs = (
        P(None, None, "rows"),
        P("rows"),
        P("rows", "heads"),
        P(),
        P("heads", "rows"),
        P(),
        P("rows", "heads", None, None, None),
        P("rows", "heads", None, None),
        P(None, "rows"),
        P(),
    )
    out_specs = (P(None, None, "rows"), P("rows", "heads", None, None))
    return jax.shard_map(
        on_device, mesh=mesh, in_specs=in_specs, out_specs=out_specs, check_vma=False
    )
```

profile of v0, /device:TPU:0, one launch (start us, length us, event | category | flops | bytes accessed | tf_op | source)
XLA Modules:
  0.0 437.0 jit_solution(6062758241565056148)
XLA Ops:
  7.2 0.8 convert_element_type.63
  8.1 3.8 fusion.31
  11.8 1.4 fusion.34
  16.5 4.4 %select_bitcast_fusion.1 = (bf16[4,1408,256]{2,1,0:T(8,128)(2,1)}, bf16[4,1408,256]{2,1,0:T(8,128)(2,1)}, bf16[4,1408,256]{2,1,0:T(8,128)(2,1)}, bf16[4,1408,256]{2,1,0:T(8,128)(2,1)}) fusion(bf16[1,4,1408,256]{3,2,1,0:T(8,128)(2,1)S(1)} %copy-done.6, pred[]{:T(512)S(6)} %eq.15, pred[]{:T(512)S(6)} %eq.13, pred[]{:T(512)S(6)} %eq.12, pred[]{:T(512)S(6)} %eq.14), kind=kLoop, calls=%fused_computation.27 | loop fusion | flops 5767168 | bytes 14417924 | tf_op jit(solution)/shard_map/jit(_where)/select_n | solution.py:16
  28.7 9.9 %copy.23 = bf16[1,4,4,1408,256]{4,3,1,2,0:T(8,128)(2,1)} copy(bf16[1,4,4,1408,256]{4,3,2,1,0:T(8,128)(2,1)} %param.16) | data formatting | bytes 23068672 | tf_op args[6]
  44.4 61.7 %all-reduce.9.cloned.1.call-done = (f32[16,4096]{1,0:T(8,128)}, f32[16,4096]{1,0:T(8,128)}) async-done(((f32[16,4096]{1,0:T(8,128)}, f32[16,4096]{1,0:T(8,128)}), (f32[16,4096]{1,0:T(8,128)}, f32[16,4096]{1,0:T(8,128)})) %all-reduce.9.cloned.1.call-update) | async-done | bytes 524304
  106.1 1.7 fusion.46
  108.2 222.0 %all-reduce.13.cloned.1.call-done = (bf16[4,1408,256]{2,1,0:T(8,128)(2,1)}, bf16[4,1408,256]{2,1,0:T(8,128)(2,1)}, bf16[4,1408,256]{2,1,0:T(8,128)(2,1)}, bf16[4,1408,256]{2,1,0:T(8,128)(2,1)}) async-done(((bf16[4,1408,256]{2,1,0:T(8,128)(2,1)}, bf16[4,1408,256]{2,1,0:T(8,128)(2,1)}, bf16[4,1408,256]{2,1,0:T(8,128)(2,1)}, bf16[4,1408,256]{2,1,0:T(8,128)(2,1)}), (bf16[4,1408,256]{2,1,0:T(8,128)(2,1)}, ...) | async-done | bytes 11534352 | tf_op jit(solution)/shard_map/psum | solution.py:17
  330.2 5.1 %fusion.15 = bf16[1,4,4,1408,256]{4,3,1,2,0:T(8,128)(2,1)} fusion(bf16[1,4,4,1408,256]{4,3,1,2,0:T(8,128)(2,1)} %copy.23, s32[]{:T(128)S(6)} %select_n.141, bf16[4,1408,256]{2,1,0:T(8,128)(2,1)} %get-tuple-element.6, pred[]{:T(512)S(6)} %and.17), kind=kLoop, calls=%fused_computation.25 | loop fusion | flops 1441792 | bytes 8650757 | tf_op jit(solution)/shard_map/dynamic_update_slice | solution.py:28
  335.3 4.3 fusion.14
  339.6 5.9 %copy.24 = bf16[1,4,4,1408,256]{4,3,2,1,0:T(8,128)(2,1)S(1)} copy(bf16[1,4,4,1408,256]{4,3,1,2,0:T(8,128)(2,1)} %fusion.14) | data formatting | bytes 23068672 | tf_op jit(solution)/shard_map/dynamic_update_slice | solution.py:28
  345.4 1.6 fusion.5
  347.4 0.9 fusion.16
  348.4 21.0 %all-gather = bf16[16,1,4096]{2,1,0:T(2,128)(2,1)S(1)} all-gather(bf16[1,1,4096]{2,1,0:T(2,128)(2,1)S(1)} %reshape.262), channel_id=1, replica_groups=mesh['rows'=16,'heads'=2] {'rows'}, dimensions={0}, use_global_device_ids=true | all-gather | bytes 139264 | tf_op jit(solution)/shard_map/all_gather | solution.py:108
  369.4 4.2 fusion.13
  373.6 4.2 fusion.12
  377.8 5.9 %copy.25 = bf16[1,4,4,1408,256]{4,3,2,1,0:T(8,128)(2,1)S(1)} copy(bf16[1,4,4,1408,256]{4,3,1,2,0:T(8,128)(2,1)} %fusion.12) | data formatting | bytes 23068672 | tf_op jit(solution)/shard_map/dynamic_update_slice | solution.py:28
  383.7 1.6 fusion.4
  385.7 0.9 fusion.17
  386.7 18.3 %all-gather.1 = bf16[16,1,4096]{2,1,0:T(2,128)(2,1)S(1)} all-gather(bf16[1,1,4096]{2,1,0:T(2,128)(2,1)S(1)} %reshape.264), channel_id=1, replica_groups=mesh['rows'=16,'heads'=2] {'rows'}, dimensions={0}, use_global_device_ids=true | all-gather | bytes 139264 | tf_op jit(solution)/shard_map/all_gather | solution.py:108
  404.9 3.4 fusion.23
  408.4 1.3 fusion.20
  410.2 2.1 select_bitcast_fusion
  412.3 16.8 %all-reduce.11.cloned.1.call-done = (f32[16,512]{1,0:T(8,128)}, f32[16,512]{1,0:T(8,128)}) async-done(((f32[16,512]{1,0:T(8,128)}, f32[16,512]{1,0:T(8,128)}), (f32[16,512]{1,0:T(8,128)}, f32[16,512]{1,0:T(8,128)})) %all-reduce.11.cloned.1.call-update) | async-done | bytes 65552 | tf_op jit(solution)/shard_map/psum | solution.py:112
  (48 shorter events, 5.3 us)
Async XLA Ops:
  7.2 4.7 %copy-start.7 = (bf16[2,16,512]{2,1,0:T(8,128)(2,1)S(1)}, bf16[2,16,512]{2,1,0:T(8,128)(2,1)}, u32[]{:S(2)}) copy-start(bf16[2,16,512]{2,1,0:T(8,128)(2,1)} %param.10) | copy-start | bytes 98308
  7.2 98.9 %all-reduce.9.cloned.1.call-start = ((), (), s32[]{:S(2)}) async-start(), calls=%async_computation | async-start | bytes 1048576
  7.2 4.6 %copy-start = (bf16[512,4096]{1,0:T(8,128)(2,1)S(1)}, bf16[512,4096]{1,0:T(8,128)(2,1)}, u32[]{:S(2)}) copy-start(bf16[512,4096]{1,0:T(8,128)(2,1)} %param.12) | copy-start | bytes 12582916
  11.8 1.5 copy-start.8
  11.8 4.7 %copy-start.6 = (bf16[1,4,1408,256]{3,2,1,0:T(8,128)(2,1)S(1)}, bf16[1,4,1408,256]{3,2,1,0:T(8,128)(2,1)}, u32[]{:S(2)}) copy-start(bf16[1,4,1408,256]{3,2,1,0:T(8,128)(2,1)} %param.17) | copy-start | bytes 8650756
  13.2 317.0 %all-reduce.13.cloned.1.call-start = ((), (), s32[]{:S(2)}) async-start(), calls=%async_computation.2 | async-start | bytes 23068672 | tf_op jit(solution)/shard_map/psum | solution.py:17
  21.0 408.1 %all-reduce.11.cloned.1.call-start = ((), (), s32[]{:S(2)}) async-start(), calls=%async_computation.1 | async-start | bytes 131072 | tf_op jit(solution)/shard_map/psum | solution.py:112
  28.6 10.0 %copy-start.10 = (bf16[128]{0:T(256)(128)(2,1)S(1)}, bf16[128]{0:T(256)(128)(2,1)}, u32[]{:S(2)}) copy-start(bf16[128]{0:T(256)(128)(2,1)} %param.13) | copy-start | bytes 772
  28.7 10.0 %copy-start.9 = (s32[2,1]{0,1:T(1,128)S(1)}, s32[2,1]{0,1:T(1,128)}, u32[]{:S(2)}) copy-start(s32[2,1]{0,1:T(1,128)} %param.18) | copy-start | bytes 28
  28.7 13.8 %copy-start.11 = (u32[32]{0:T(128)S(1)}, u32[32]{0:T(128)}, u32[]{:S(2)}) copy-start(u32[32]{0:T(128)} %constant.50) | copy-start | bytes 388
  330.2 5.1 %copy-start.3 = (bf16[4,1408,256]{2,1,0:T(8,128)(2,1)S(1)}, bf16[4,1408,256]{2,1,0:T(8,128)(2,1)}, u32[]{:S(2)}) copy-start(bf16[4,1408,256]{2,1,0:T(8,128)(2,1)} %get-tuple-element.7) | copy-start | bytes 8650756
  347.4 21.9 %copy-start.4 = (bf16[4,1408,256]{2,1,0:T(8,128)(2,1)S(1)}, bf16[4,1408,256]{2,1,0:T(8,128)(2,1)}, u32[]{:S(2)}) copy-start(bf16[4,1408,256]{2,1,0:T(8,128)(2,1)} %get-tuple-element.8) | copy-start | bytes 8650756
  369.4 4.2 copy-start.5
  386.6 21.7 %copy-start.1 = (bf16[4096,512]{1,0:T(8,128)(2,1)S(1)}, bf16[4096,512]{1,0:T(8,128)(2,1)}, u32[]{:S(2)}) copy-start(bf16[4096,512]{1,0:T(8,128)(2,1)} %param.14) | copy-start | bytes 12582916
  408.4 1.8 copy-start.2
Sparse Core Ops, SparseCore 0:
  13.4 92.6 all-reduce.8
  110.8 219.3 all-reduce.12
  409.8 19.2 all-reduce.10
where the time goes:
time: 438 us; the launch traced here: 437 us
  waiting for transfers between devices  301 us (69%)
  blocking collectives  39.3 us (9%)
  other arithmetic  29.2 us (7%)
  between operations  28.6 us (7%)
  local copies, waits for them, and re-layouts  24.3 us (6%)
  matrix products  15 us (3%)
    psum x1, waiting for transfers between devices, broadcast(): return lax.psum(block, axis)  222 us
    unnamed x4, waiting for transfers between devices  61.7 us
    all_gather x2, blocking collectives, on_device(): lax.all_gather(context, 'rows', axis=0, tiled=True)  39.3 us
    dynamic_update_slice x4, other arithmetic, place_tile(): lax.dynamic_update_slice(kv_state, updated, (row_index, anchor, slot_inde...  17.8 us
    psum x1, waiting for transfers between devices, on_device(): projected = lax.psum(partial_value, 'heads')  16.8 us
    dynamic_update_slice x2, local copies, waits for them, and re-layouts, place_tile(): lax.dynamic_update_slice(kv_state, updated, (row_index, anchor, slot_inde...  11.7 us
    unnamed x28, local copies, waits for them, and re-layouts  11.2 us
  transfers between devices with their start and end apart: 3, of which 3 were waited for; matrix products, arithmetic and copies ran while one was open for 5% of the time, Pallas kernels for 0%

commit v1 on v0

v1 whole, which is shorter than its diff:
```python
import functools
import math

import jax
import jax.numpy as jnp
from jax import lax
from jax.experimental import pallas as pl
from jax.experimental.pallas import tpu as pltpu
from jax.sharding import PartitionSpec as P

STEPS = 2
JOINS = 2
TOTAL = STEPS * JOINS

epsilon = 1e-05

ROUNDS = [(0, 0, 0, 0), (0, 1, 0, 0), (0, 0, 1, 0), (0, 0, 0, 1),
          (0, 1, 1, 0), (0, 1, 0, 1), (0, 0, 1, 1), (0, 1, 1, 1)]


def plan_kernel(join_ref, plan_ref):
    me = lax.axis_index("rows")
    source, target, slot = [], [], []
    for s in range(STEPS):
        for j in range(JOINS):
            source.append(join_ref[s, j, 0])
            target.append(join_ref[s, j, 1])
            slot.append(join_ref[s, j, 2])
    one, zero = jnp.int32(1), jnp.int32(0)
    clash = {}
    for i in range(TOTAL):
        for j in range(i + 1, TOTAL):
            both = (source[i] == target[j]) | (source[j] == target[i])
            clash[i, j] = jnp.where(both, one, zero)
    best = [jnp.int32(0)] * TOTAL
    found = zero
    for rounds in reversed(ROUNDS):
        bad = zero
        for (i, j), value in clash.items():
            if rounds[i] == rounds[j]:
                bad = bad | value
        good = bad == 0
        found = jnp.where(good, one, found)
        best = [jnp.where(good, jnp.int32(r), b) for r, b in zip(rounds, best)]
    odd = found == 0
    branch = [zero, zero]
    arrives, step, place = zero, jnp.int32(STEPS), zero
    for i in range(TOTAL):
        s, t = source[i], target[i]
        key = s ^ t
        kind = jnp.where(key == 0, 1, 2 + 2 * (key - 1) + jnp.where(s < t, 0, 1))
        part = (me == s) | (me == t)
        for r in range(2):
            branch[r] = jnp.where(part & (best[i] == r), kind, branch[r])
        here = me == t
        arrives = jnp.where(here, best[i] + 1, arrives)
        step = jnp.where(here, i // JOINS, step)
        place = jnp.where(here, slot[i], place)
    plan_ref[0] = jnp.where(odd, zero, branch[0])
    plan_ref[1] = jnp.where(odd, zero, branch[1])
    plan_ref[2] = jnp.where(odd & (arrives > 0), jnp.int32(1), arrives)
    plan_ref[3] = step
    plan_ref[4] = place
    plan_ref[5] = jnp.where(odd, one, zero)


def make_plan(join_list, rows):
    last = 2 + 2 * (rows - 1)
    plan = pl.pallas_call(
        plan_kernel,
        out_shape=jax.ShapeDtypeStruct((8,), jnp.int32),
        in_specs=[pl.BlockSpec(memory_space=pltpu.SMEM)],
        out_specs=pl.BlockSpec(memory_space=pltpu.SMEM),
        name="plan",
    )(join_list)
    return plan, last


def transfer(tile, branch, rows, extra=None):
    def skip(block):
        return jnp.zeros_like(block)

    def keep(block):
        return block

    def send(pairs):
        return lambda block: lax.ppermute(block, "rows", pairs)

    branches = [skip, keep]
    for key in range(1, rows):
        for low in (True, False):
            pairs = [(i, i ^ key) for i in range(rows) if (i < (i ^ key)) == low]
            branches.append(send(pairs))
    if extra is not None:
        branches.append(extra)
    return lax.switch(branch, branches, tile)


def attend_kernel(parts, group, head_size, plan_ref, counts_ref, gain_ref, *refs):
    sums, (kv_ref, new_ref, out_ref) = refs[:parts], refs[parts:]
    slots = kv_ref.shape[2]
    raw = sums[0][...]
    for ref in sums[1:]:
        raw = raw + ref[...]
    raw = jnp.concatenate(
        [raw[:, g * head_size:(g + 1) * head_size] for g in range(group)], axis=0
    )
    queries = (
        raw
        * lax.rsqrt(jnp.mean(raw * raw, axis=-1, keepdims=True) + epsilon)
        * gain_ref[...].astype(jnp.float32)
    ).astype(jnp.bfloat16)
    row = lax.broadcasted_iota(jnp.int32, (group * STEPS, 1), 0)
    second = lax.rem(row, STEPS) == 1
    join_step, join_slot = plan_ref[3], plan_ref[4]
    one, zero = jnp.int32(1), jnp.int32(0)

    def scores_of(keys, shown):
        scores = lax.dot_general(
            queries, keys, (((1,), (1,)), ((), ())), preferred_element_type=jnp.float32
        ) * (1.0 / math.sqrt(head_size))
        usable = jnp.where(second, shown[1], shown[0]) > 0
        return jnp.where(usable, scores, -1e30)

    all_scores = []
    for i in range(slots):
        shown = [
            jnp.where(
                (i < counts_ref[s, 0]) & ((join_step > s) | (join_slot != i)), one, zero
            )
            for s in range(STEPS)
        ]
        all_scores.append(scores_of(kv_ref[0, 0, i, :, :head_size], shown))
    shown = [jnp.where(join_step <= s, one, zero) for s in range(STEPS)]
    all_scores.append(scores_of(new_ref[0, :, :head_size], shown))
    highest = all_scores[0].max(axis=-1, keepdims=True)
    for scores in all_scores[1:]:
        highest = jnp.maximum(highest, scores.max(axis=-1, keepdims=True))
    exponents = [jnp.exp(scores - highest) for scores in all_scores]
    total = exponents[0].sum(axis=-1, keepdims=True)
    for exponent in exponents[1:]:
        total = total + exponent.sum(axis=-1, keepdims=True)
    context = jnp.zeros((group * STEPS, head_size), jnp.float32)
    for i in range(slots + 1):
        probs = (exponents[i] / total).astype(jnp.bfloat16)
        values = new_ref[0, :, head_size:] if i == slots else kv_ref[0, 0, i, :, head_size:]
        context = context + jnp.dot(probs, values, preferred_element_type=jnp.float32)
    context = jnp.concatenate(
        [context[g * STEPS:(g + 1) * STEPS] for g in range(group)], axis=1
    )
    out_ref[...] = context.astype(jnp.bfloat16)


def attend(plan, counts, query_gain, sums, kv_cache, arrived):
    _, kv_here, slots, tile_len, width = kv_cache.shape
    head_size = width // 2
    heads_here = sums[0].shape[1] // head_size
    group = heads_here // kv_here
    wide = group * head_size
    smem = pl.BlockSpec(memory_space=pltpu.SMEM)
    return pl.pallas_call(
        functools.partial(attend_kernel, len(sums), group, head_size),
        grid=(kv_here,),
        out_shape=jax.ShapeDtypeStruct((STEPS, heads_here * head_size), jnp.bfloat16),
        in_specs=[smem, smem, pl.BlockSpec((1, head_size), lambda h: (0, 0))]
        + [pl.BlockSpec((STEPS, wide), lambda h: (0, h)) for _ in sums]
        + [
            pl.BlockSpec((1, 1, slots, tile_len, width), lambda h: (0, h, 0, 0, 0)),
            pl.BlockSpec((1, tile_len, width), lambda h: (h, 0, 0)),
        ],
        out_specs=pl.BlockSpec((STEPS, wide), lambda h: (0, h)),
        compiler_params=pltpu.CompilerParams(vmem_limit_bytes=40 * 1024 * 1024),
        cost_estimate=pl.CostEstimate(
            flops=4 * kv_here * (slots + 1) * tile_len * width * group,
            bytes_accessed=kv_here * (slots + 1) * tile_len * width * 2,
            transcendentals=kv_here * (slots + 1) * tile_len * group * STEPS,
        ),
        name="attend",
    )(plan, counts, query_gain.reshape(1, head_size), *sums, kv_cache, arrived)


def on_device(
    rows,
    heads,
    hidden,
    norm_gain,
    query_weight,
    query_gain,
    out_weight,
    attn_gate,
    kv_cache,
    new_tiles,
    counts,
    join_list,
):
    width = hidden.shape[2]
    me = lax.axis_index("rows")
    chips = rows // 2
    own_tile = new_tiles[0]
    plan, last = make_plan(join_list, rows)

    order = jnp.arange(rows, dtype=jnp.int32) ^ me
    shuffle = (order[:, None] == jnp.arange(rows, dtype=jnp.int32)[None, :])
    shuffle = shuffle.astype(jnp.bfloat16)
    wide_hidden = hidden.astype(jnp.float32)
    scaled = (wide_hidden * norm_gain.astype(jnp.float32)).astype(jnp.bfloat16)
    scaled = jnp.einsum(
        "kb,sbd->ksd", shuffle, scaled, preferred_element_type=jnp.float32
    ).astype(jnp.bfloat16)
    partial = jnp.dot(
        scaled.reshape(rows * STEPS, width), query_weight, preferred_element_type=jnp.float32
    )
    columns = partial.shape[1]
    partial = partial.reshape(chips, 2, STEPS, columns)

    def across(block, axis, size, key):
        return lax.ppermute(block, axis, [(i, i ^ key) for i in range(size)])

    pair = partial[:, 0] + across(partial[:, 1], "rows", rows, 1)
    sums = [pair[0]] + [across(pair[k], "rows", rows, 2 * k) for k in range(1, chips)]

    def summed(block):
        result = jnp.zeros_like(block)
        for s in range(STEPS):
            for j in range(JOINS):
                given = jnp.where(me == join_list[s, j, 0], block, jnp.zeros_like(block))
                given = lax.psum(given, "rows")
                result = jnp.where(me == join_list[s, j, 1], given, result)
        return result

    first = transfer(
        own_tile, jnp.where(plan[5] > 0, last, plan[0]), rows, summed
    )
    other = transfer(own_tile, plan[1], rows)
    arrived = jnp.where(
        plan[2] == 1, first, jnp.where(plan[2] == 2, other, jnp.zeros_like(own_tile))
    )
    context = attend(plan, counts, query_gain, sums, kv_cache, arrived)
    gathered = jnp.stack(
        [context] + [across(context, "rows", rows, 2 * k) for k in range(1, chips)]
    )
    gathered = jnp.stack([gathered, across(gathered, "rows", rows, 1)], axis=1)
    gathered = gathered.reshape(rows * STEPS, columns)
    projected = jnp.dot(gathered, out_weight, preferred_element_type=jnp.float32)
    key = 1
    while key < heads:
        projected = projected + across(projected, "heads", heads, key)
        key *= 2
    projected = projected.reshape(rows, STEPS, width)
    bit = 1
    while bit < rows:
        split = projected.reshape(rows // (2 * bit), 2, bit, STEPS, width)
        projected = jnp.where((me & bit) > 0, split[:, ::-1], split)
        bit *= 2
    projected = projected.reshape(rows, STEPS, width).transpose(1, 0, 2)
    mixed = (wide_hidden + jnp.tanh(attn_gate[0]) * projected).astype(jnp.bfloat16)
    return mixed, arrived[None]


def solution(mesh):
    in_specs = (
        P(None, None, "rows"),
        P("rows"),
        P("rows", "heads"),
        P(),
        P("heads", "rows"),
        P(),
        P("rows", "heads", None, None, None),
        P("rows", "heads", None, None),
        P(None, "rows"),
        P(),
    )
    out_specs = (P(None, None, "rows"), P("rows", "heads", None, None))
    body = functools.partial(on_device, mesh.shape["rows"], mesh.shape["heads"])
    return jax.shard_map(
        body, mesh=mesh, in_specs=in_specs, out_specs=out_specs, check_vma=False
    )
```

time: 438 us -> 163 us (0.37)
  waiting for transfers between devices: 301 us -> 17.2 us
  starting transfers between devices: 0.12 us -> 101 us
  blocking collectives: 39.3 us -> 0 us
  other arithmetic: 29.2 us -> 2.37 us
  local copies, waits for them, and re-layouts: 24.3 us -> 6.92 us
  between operations: 28.6 us -> 18.2 us
  Pallas kernels: 0 us -> 8.86 us
  matrix products: 15 us -> 7.08 us
    psum x2 -> x0, waiting for transfers between devices: 239 us -> none  [the longest x1 222 us: broadcast(): return lax.psum(block, axis)]
    ppermute x0 -> x17, starting transfers between devices: none -> 101 us  [across(): return lax.ppermute(block, axis, [(i, i ^ key) for i in range(size)])]
    unnamed x4 -> x0, waiting for transfers between devices: 61.7 us -> none
    all_gather x2 -> x0, blocking collectives: 39.3 us -> none  [on_device(): lax.all_gather(context, 'rows', axis=0, tiled=True)]
    dynamic_update_slice x4 -> x0, other arithmetic: 17.8 us -> none  [place_tile(): lax.dynamic_update_slice(kv_state, updated, (row_index, anchor, slot_inde...]
    ppermute x0 -> x17, waiting for transfers between devices: none -> 17.2 us  [across(): return lax.ppermute(block, axis, [(i, i ^ key) for i in range(size)])]
    dynamic_update_slice x2 -> x0, local copies, waits for them, and re-layouts: 11.7 us -> none  [place_tile(): lax.dynamic_update_slice(kv_state, updated, (row_index, anchor, slot_inde...]
    unnamed x28 -> x23, local copies, waits for them, and re-layouts: 11.2 us -> 1.48 us
  transfers between devices with their start and end apart: 3 -> 17, of which waited for: 3 -> 5; matrix products, arithmetic and copies ran while one was open for 5% -> 3% of each run, Pallas kernels for 0% -> 1%
where the time goes in v1:
time: 163 us; the launch traced here: 161 us
  starting transfers between devices  101 us (62%)
  between operations  18.2 us (11%)
  waiting for transfers between devices  17.2 us (11%)
  Pallas kernels  8.86 us (5%)
  matrix products  7.08 us (4%)
  local copies, waits for them, and re-layouts  6.92 us (4%)
  other arithmetic  2.37 us (1%)
    ppermute x17, starting transfers between devices, across(): return lax.ppermute(block, axis, [(i, i ^ key) for i in range(size)])  101 us
    ppermute x17, waiting for transfers between devices, across(): return lax.ppermute(block, axis, [(i, i ^ key) for i in range(size)])  17.2 us
    pallas_call x1, Pallas kernels, attend(): pl.pallas_call(functools.partial(attend_kernel, len(sums), group, head_si...  7.72 us
    another operation x2, local copies, waits for them, and re-layouts  3.5 us
  transfers between devices with their start and end apart: 17, of which 5 were waited for; matrix products, arithmetic and copies ran while one was open for 3% of the time, Pallas kernels for 1%

profile of v1, /device:TPU:0, one launch (start us, length us, event | category | flops | bytes accessed | tf_op | source)
XLA Modules:
  0.0 161.1 jit_solution(9102044497051136727)
XLA Ops:
  8.9 3.1 %fusion = f32[8,2,2,4096]{3,0,2,1:T(8,128)S(1)} fusion(bf16[512,4096]{1,0:T(8,128)(2,1)} %param.77, bf16[8,2,2,512]{3,1,0,2:T(2,128)(2,1)S(1)} %dot_general.12), kind=kOutput, calls=%fused_computation.5 | convolution fusion | flops 134217728 | bytes 4751360 | tf_op jit(solution)/shard_map/dot_general | solution.py:210
  13.4 1.1 plan.1.plan_ref
  15.1 2.9 %collective-permute-start.61 = (f32[2,4096]{1,0:T(2,128)S(1)}, f32[2,4096]{1,0:T(2,128)S(1)}, u32[]{:S(2)}, u32[]{:S(2)}) collective-permute-start(f32[2,4096]{1,0:T(2,128)S(1)} %get-tuple-element.164), channel_id=1, source_target_pairs={{0,4},{2,6},{4,0},{6,2},{8,12},{10,14},{12,8},{14,10},{16,20},{18,... | collective-permute-start | bytes 98312 | tf_op jit(solution)/shard_map/ppermute | solution.py:217
  18.0 1.6 collective-permute-start.62
  19.6 1.5 fusion.15
  24.2 1.8 %conditional.3 = (bf16[4,1408,256]{2,1,0:T(8,128)(2,1)}) conditional(s32[]{:T(128)} %bitcast.27, () %tuple.205, bf16[4,1408,256]{2,1,0:T(8,128)(2,1)S(1)} %bitcast.81, bf16[4,1408,256]{2,1,0:T(8,128)(2,1)S(1)} %bitcast.82, bf16[4,1408,256]{2,1,0:T(8,128)(2,1)S(1)} %bitcast.83, ...), branch_computations={%region_37.38_spmd, %region_38.39_spmd, %region_39.40_spmd, %regio... | conditional | bytes 11534384 | solution.py:96
  24.2 1.8 %broadcast.19 = bf16[4,1408,256]{2,1,0:T(8,128)(2,1)} broadcast(bf16[]{:T(256)} %constant.14.clone), dimensions={} | broadcast | bytes 2883586 | tf_op jit(solution)/shard_map/broadcast.6
  26.0 1.7 %conditional.2 = (bf16[4,1408,256]{2,1,0:T(8,128)(2,1)}) conditional(s32[]{:T(128)} %bitcast.24, () %tuple.203, bf16[4,1408,256]{2,1,0:T(8,128)(2,1)S(1)} %bitcast.112, bf16[4,1408,256]{2,1,0:T(8,128)(2,1)S(1)} %bitcast.113, bf16[4,1408,256]{2,1,0:T(8,128)(2,1)S(1)} %bitcast.114, ...), branch_computations={%region_0.1_spmd, %region_1.2_spmd, %region_2.3_spmd, %region_3.4_... | conditional | flops 17301512 | bytes 98042040 | solution.py:96
  26.0 1.7 %broadcast.17 = bf16[4,1408,256]{2,1,0:T(8,128)(2,1)} broadcast(bf16[]{:T(256)} %constant.10.clone), dimensions={} | broadcast | bytes 2883586 | tf_op jit(solution)/shard_map/broadcast.2
  27.7 34.7 %collective-permute-start.63 = (f32[2,4096]{1,0:T(2,128)S(1)}, f32[2,4096]{1,0:T(2,128)S(1)}, u32[]{:S(2)}, u32[]{:S(2)}) collective-permute-start(f32[2,4096]{1,0:T(2,128)S(1)} %get-tuple-element.162), channel_id=1, source_target_pairs={{0,12},{2,14},{4,8},{6,10},{8,4},{10,6},{12,0},{14,2},{16,28},{18,... | collective-permute-start | bytes 98312 | tf_op jit(solution)/shard_map/ppermute | solution.py:217
  62.4 33.7 %collective-permute-start.64 = (f32[2,4096]{1,0:T(2,128)S(1)}, f32[2,4096]{1,0:T(2,128)S(1)}, u32[]{:S(2)}, u32[]{:S(2)}) collective-permute-start(f32[2,4096]{1,0:T(2,128)S(1)} %get-tuple-element.161), channel_id=1, source_target_pairs={{0,16},{2,18},{4,20},{6,22},{8,24},{10,26},{12,28},{14,30},{16,0},... | collective-permute-start | bytes 98312 | tf_op jit(solution)/shard_map/ppermute | solution.py:217
  96.1 4.9 %collective-permute-start.66 = (f32[2,4096]{1,0:T(2,128)S(1)}, f32[2,4096]{1,0:T(2,128)S(1)}, u32[]{:S(2)}, u32[]{:S(2)}) collective-permute-start(f32[2,4096]{1,0:T(2,128)S(1)} %get-tuple-element.159), channel_id=1, source_target_pairs={{0,24},{2,26},{4,28},{6,30},{8,16},{10,18},{12,20},{14,22},{16,8},... | collective-permute-start | bytes 98312 | tf_op jit(solution)/shard_map/ppermute | solution.py:217
  101.0 5.7 %collective-permute-start.67 = (f32[2,4096]{1,0:T(2,128)S(1)}, f32[2,4096]{1,0:T(2,128)S(1)}, u32[]{:S(2)}, u32[]{:S(2)}) collective-permute-start(f32[2,4096]{1,0:T(2,128)S(1)} %get-tuple-element.158), channel_id=1, source_target_pairs={{0,28},{2,30},{4,24},{6,26},{8,20},{10,22},{12,16},{14,18},{16,12}... | collective-permute-start | bytes 98312 | tf_op jit(solution)/shard_map/ppermute | solution.py:217
  107.5 5.8 %collective-permute-done.67.refs_7_ = f32[2,4096]{1,0:T(2,128)S(1)} collective-permute-done((f32[2,4096]{1,0:T(2,128)S(1)}, f32[2,4096]{1,0:T(2,128)S(1)}, u32[]{:S(2)}, u32[]{:S(2)}) %collective-permute-start.67) | collective-permute-done | bytes 32800 | tf_op jit(solution)/shard_map/ppermute | solution.py:217
  113.3 7.7 %attend.1 = bf16[2,4096]{1,0:T(2,128)(2,1)S(1)} custom-call(s32[8]{0:T(128)S(1)} %copy-done.1, s32[2,1]{1,0:T(2,128)S(1)} %copy.21.counts_ref, bf16[1,128]{1,0:T(2,128)(2,1)S(1)} %bitcast.80, f32[2,4096]{1,0:T(2,128)S(1)} %get-tuple-element.165.refs_0_, f32[2,4096]{1,0:T(2,128)S(1)} %collective-permute-done.61.refs_1_, ...), custom_call_target="tpu_custom_call" | custom-call | flops 230686720 | bytes 14417920 | tf_op jit(solution)/shard_map/attend/pallas_call | solution.py:161
  121.7 2.9 %collective-permute-start.70 = (bf16[2,4096]{1,0:T(2,128)(2,1)S(1)}, bf16[2,4096]{1,0:T(2,128)(2,1)S(1)}, u32[]{:S(2)}, u32[]{:S(2)}) collective-permute-start(bf16[2,4096]{1,0:T(2,128)(2,1)S(1)} %attend.1), channel_id=1, source_target_pairs={{0,12},{2,14},{4,8},{6,10},{8,4},{10,6},{12,0},{14,2},{16,28},{18,... | collective-permute-start | bytes 49160 | tf_op jit(solution)/shard_map/ppermute | solution.py:217
  124.8 2.8 %collective-permute-start.72 = (bf16[2,4096]{1,0:T(2,128)(2,1)S(1)}, bf16[2,4096]{1,0:T(2,128)(2,1)S(1)}, u32[]{:S(2)}, u32[]{:S(2)}) collective-permute-start(bf16[2,4096]{1,0:T(2,128)(2,1)S(1)} %attend.1), channel_id=1, source_target_pairs={{0,20},{2,22},{4,16},{6,18},{8,28},{10,30},{12,24},{14,26},{16,4},... | collective-permute-start | bytes 49160 | tf_op jit(solution)/shard_map/ppermute | solution.py:217
  127.6 2.5 %collective-permute-start.73 = (bf16[2,4096]{1,0:T(2,128)(2,1)S(1)}, bf16[2,4096]{1,0:T(2,128)(2,1)S(1)}, u32[]{:S(2)}, u32[]{:S(2)}) collective-permute-start(bf16[2,4096]{1,0:T(2,128)(2,1)S(1)} %attend.1), channel_id=1, source_target_pairs={{0,24},{2,26},{4,28},{6,30},{8,16},{10,18},{12,20},{14,22},{16,8},... | collective-permute-start | bytes 49160 | tf_op jit(solution)/shard_map/ppermute | solution.py:217
  130.2 5.8 %collective-permute-start.74 = (bf16[2,4096]{1,0:T(2,128)(2,1)S(1)}, bf16[2,4096]{1,0:T(2,128)(2,1)S(1)}, u32[]{:S(2)}, u32[]{:S(2)}) collective-permute-start(bf16[2,4096]{1,0:T(2,128)(2,1)S(1)} %attend.1), channel_id=1, source_target_pairs={{0,28},{2,30},{4,24},{6,26},{8,20},{10,22},{12,16},{14,18},{16,12}... | collective-permute-start | bytes 49160 | tf_op jit(solution)/shard_map/ppermute | solution.py:217
  136.1 6.2 %collective-permute-done.74 = bf16[2,4096]{1,0:T(2,128)(2,1)S(1)} collective-permute-done((bf16[2,4096]{1,0:T(2,128)(2,1)S(1)}, bf16[2,4096]{1,0:T(2,128)(2,1)S(1)}, u32[]{:S(2)}, u32[]{:S(2)}) %collective-permute-start.74) | collective-permute-done | bytes 16416 | tf_op jit(solution)/shard_map/ppermute | solution.py:217
  142.4 1.3 collective-permute-done.75
  144.5 3.0 %fusion.16 = f32[32,512]{1,0:T(8,128)S(1)} fusion(bf16[32,4096]{1,0:T(8,128)(2,1)S(1)} %reshape.47, bf16[4096,512]{1,0:T(8,128)(2,1)} %param.79), kind=kOutput, calls=%fused_computation.48 | convolution fusion | flops 134217728 | bytes 4521984 | tf_op jit(solution)/shard_map/dot_general | solution.py:244
  147.5 1.6 %collective-permute-start.76 = (f32[32,512]{1,0:T(8,128)S(1)}, f32[32,512]{1,0:T(8,128)S(1)}, u32[]{:S(2)}, u32[]{:S(2)}) collective-permute-start(f32[32,512]{1,0:T(8,128)S(1)} %fusion.16), channel_id=1, source_target_pairs={{0,1},{1,0},{2,3},{3,2},{4,5},{5,4},{6,7},{7,6},{8,9},{9,8},{10,11... | collective-permute-start | bytes 196616 | tf_op jit(solution)/shard_map/ppermute | solution.py:217
  149.8 3.6 %collective-permute-done.76 = f32[32,512]{1,0:T(8,128)S(1)} collective-permute-done((f32[32,512]{1,0:T(8,128)S(1)}, f32[32,512]{1,0:T(8,128)S(1)}, u32[]{:S(2)}, u32[]{:S(2)}) %collective-permute-start.76) | collective-permute-done | bytes 65568 | tf_op jit(solution)/shard_map/ppermute | solution.py:217
  (62 shorter events, 6.8 us)
Async XLA Ops:
  8.8 4.6 %copy-start.5 = (s32[2,2,3]{2,1,0:T(2,128)S(1)}, s32[2,2,3]{2,1,0:T(2,128)}, u32[]{:S(2)}) copy-start(s32[2,2,3]{2,1,0:T(2,128)} %join_ref.1) | copy-start | bytes 148
  8.8 15.3 %copy-start.3 = (bf16[1,4,1408,256]{3,2,1,0:T(8,128)(2,1)S(1)}, bf16[1,4,1408,256]{3,2,1,0:T(8,128)(2,1)}, u32[]{:S(2)}) copy-start(bf16[1,4,1408,256]{3,2,1,0:T(8,128)(2,1)} %param.82) | copy-start | bytes 8650756
  12.9 1.8 %collective-permute-start.60 = (f32[8,2,4096]{2,1,0:T(2,128)}, f32[8,2,4096]{2,1,0:T(2,128)S(1)}, u32[]{:S(2)}, u32[]{:S(2)}) collective-permute-start(f32[8,2,4096]{2,1,0:T(2,128)} %bitcast.78), channel_id=1, source_target_pairs={{0,2},{2,0},{4,6},{6,4},{8,10},{10,8},{12,14},{14,12},{16,18},{18,... | collective-permute-start | bytes 786440 | tf_op jit(solution)/shard_map/ppermute | solution.py:217
  15.1 81.0 %collective-permute-start.61 = (f32[2,4096]{1,0:T(2,128)S(1)}, f32[2,4096]{1,0:T(2,128)S(1)}, u32[]{:S(2)}, u32[]{:S(2)}) collective-permute-start(f32[2,4096]{1,0:T(2,128)S(1)} %get-tuple-element.164), channel_id=1, source_target_pairs={{0,4},{2,6},{4,0},{6,2},{8,12},{10,14},{12,8},{14,10},{16,20},{18,... | collective-permute-start | bytes 98312 | tf_op jit(solution)/shard_map/ppermute | solution.py:217
  18.0 83.0 %collective-permute-start.62 = (f32[2,4096]{1,0:T(2,128)S(1)}, f32[2,4096]{1,0:T(2,128)S(1)}, u32[]{:S(2)}, u32[]{:S(2)}) collective-permute-start(f32[2,4096]{1,0:T(2,128)S(1)} %get-tuple-element.163), channel_id=1, source_target_pairs={{0,8},{2,10},{4,12},{6,14},{8,0},{10,2},{12,4},{14,6},{16,24},{18,... | collective-permute-start | bytes 98312 | tf_op jit(solution)/shard_map/ppermute | solution.py:217
  27.7 79.8 %collective-permute-start.63 = (f32[2,4096]{1,0:T(2,128)S(1)}, f32[2,4096]{1,0:T(2,128)S(1)}, u32[]{:S(2)}, u32[]{:S(2)}) collective-permute-start(f32[2,4096]{1,0:T(2,128)S(1)} %get-tuple-element.162), channel_id=1, source_target_pairs={{0,12},{2,14},{4,8},{6,10},{8,4},{10,6},{12,0},{14,2},{16,28},{18,... | collective-permute-start | bytes 98312 | tf_op jit(solution)/shard_map/ppermute | solution.py:217
  62.4 45.1 %collective-permute-start.64 = (f32[2,4096]{1,0:T(2,128)S(1)}, f32[2,4096]{1,0:T(2,128)S(1)}, u32[]{:S(2)}, u32[]{:S(2)}) collective-permute-start(f32[2,4096]{1,0:T(2,128)S(1)} %get-tuple-element.161), channel_id=1, source_target_pairs={{0,16},{2,18},{4,20},{6,22},{8,24},{10,26},{12,28},{14,30},{16,0},... | collective-permute-start | bytes 98312 | tf_op jit(solution)/shard_map/ppermute | solution.py:217
  96.1 11.4 %collective-permute-start.65 = (f32[2,4096]{1,0:T(2,128)S(1)}, f32[2,4096]{1,0:T(2,128)S(1)}, u32[]{:S(2)}, u32[]{:S(2)}) collective-permute-start(f32[2,4096]{1,0:T(2,128)S(1)} %get-tuple-element.160), channel_id=1, source_target_pairs={{0,20},{2,22},{4,16},{6,18},{8,28},{10,30},{12,24},{14,26},{16,4},... | collective-permute-start | bytes 98312 | tf_op jit(solution)/shard_map/ppermute | solution.py:217
  96.1 11.4 %collective-permute-start.66 = (f32[2,4096]{1,0:T(2,128)S(1)}, f32[2,4096]{1,0:T(2,128)S(1)}, u32[]{:S(2)}, u32[]{:S(2)}) collective-permute-start(f32[2,4096]{1,0:T(2,128)S(1)} %get-tuple-element.159), channel_id=1, source_target_pairs={{0,24},{2,26},{4,28},{6,30},{8,16},{10,18},{12,20},{14,22},{16,8},... | collective-permute-start | bytes 98312 | tf_op jit(solution)/shard_map/ppermute | solution.py:217
  101.0 12.3 %collective-permute-start.67 = (f32[2,4096]{1,0:T(2,128)S(1)}, f32[2,4096]{1,0:T(2,128)S(1)}, u32[]{:S(2)}, u32[]{:S(2)}) collective-permute-start(f32[2,4096]{1,0:T(2,128)S(1)} %get-tuple-element.158), channel_id=1, source_target_pairs={{0,28},{2,30},{4,24},{6,26},{8,20},{10,22},{12,16},{14,18},{16,12}... | collective-permute-start | bytes 98312 | tf_op jit(solution)/shard_map/ppermute | solution.py:217
  106.7 0.7 copy-start.6
  106.8 6.5 %copy-start.1 = (s32[8]{0:T(128)S(1)}, s32[8]{0:T(128)}, u32[]{:S(2)}) copy-start(s32[8]{0:T(128)} %plan.1.plan_ref) | copy-start | bytes 100
  106.8 6.5 %copy-start.2 = (bf16[128]{0:T(256)(128)(2,1)S(1)}, bf16[128]{0:T(256)(128)(2,1)}, u32[]{:S(2)}) copy-start(bf16[128]{0:T(256)(128)(2,1)} %param.78) | copy-start | bytes 772
  107.4 13.6 %copy-start = (bf16[4,1408,256]{2,1,0:T(8,128)(2,1)}, bf16[4,1408,256]{2,1,0:T(8,128)(2,1)S(1)}, u32[]{:S(2)}) copy-start(bf16[4,1408,256]{2,1,0:T(8,128)(2,1)S(1)} %select_select_fusion.1.refs_9_) | copy-start | bytes 8650756
  121.0 6.5 %collective-permute-start.68 = (bf16[2,4096]{1,0:T(2,128)(2,1)S(1)}, bf16[2,4096]{1,0:T(2,128)(2,1)S(1)}, u32[]{:S(2)}, u32[]{:S(2)}) collective-permute-start(bf16[2,4096]{1,0:T(2,128)(2,1)S(1)} %attend.1), channel_id=1, source_target_pairs={{0,4},{2,6},{4,0},{6,2},{8,12},{10,14},{12,8},{14,10},{16,20},{18,... | collective-permute-start | bytes 49160 | tf_op jit(solution)/shard_map/ppermute | solution.py:217
  121.7 8.5 %collective-permute-start.69 = (bf16[2,4096]{1,0:T(2,128)(2,1)S(1)}, bf16[2,4096]{1,0:T(2,128)(2,1)S(1)}, u32[]{:S(2)}, u32[]{:S(2)}) collective-permute-start(bf16[2,4096]{1,0:T(2,128)(2,1)S(1)} %attend.1), channel_id=1, source_target_pairs={{0,8},{2,10},{4,12},{6,14},{8,0},{10,2},{12,4},{14,6},{16,24},{18,... | collective-permute-start | bytes 49160 | tf_op jit(solution)/shard_map/ppermute | solution.py:217
  121.7 14.2 %collective-permute-start.70 = (bf16[2,4096]{1,0:T(2,128)(2,1)S(1)}, bf16[2,4096]{1,0:T(2,128)(2,1)S(1)}, u32[]{:S(2)}, u32[]{:S(2)}) collective-permute-start(bf16[2,4096]{1,0:T(2,128)(2,1)S(1)} %attend.1), channel_id=1, source_target_pairs={{0,12},{2,14},{4,8},{6,10},{8,4},{10,6},{12,0},{14,2},{16,28},{18,... | collective-permute-start | bytes 49160 | tf_op jit(solution)/shard_map/ppermute | solution.py:217
  124.7 11.3 %collective-permute-start.71 = (bf16[2,4096]{1,0:T(2,128)(2,1)S(1)}, bf16[2,4096]{1,0:T(2,128)(2,1)S(1)}, u32[]{:S(2)}, u32[]{:S(2)}) collective-permute-start(bf16[2,4096]{1,0:T(2,128)(2,1)S(1)} %attend.1), channel_id=1, source_target_pairs={{0,16},{2,18},{4,20},{6,22},{8,24},{10,26},{12,28},{14,30},{16,0},... | collective-permute-start | bytes 49160 | tf_op jit(solution)/shard_map/ppermute | solution.py:217
  124.8 11.3 %collective-permute-start.72 = (bf16[2,4096]{1,0:T(2,128)(2,1)S(1)}, bf16[2,4096]{1,0:T(2,128)(2,1)S(1)}, u32[]{:S(2)}, u32[]{:S(2)}) collective-permute-start(bf16[2,4096]{1,0:T(2,128)(2,1)S(1)} %attend.1), channel_id=1, source_target_pairs={{0,20},{2,22},{4,16},{6,18},{8,28},{10,30},{12,24},{14,26},{16,4},... | collective-permute-start | bytes 49160 | tf_op jit(solution)/shard_map/ppermute | solution.py:217
  127.6 8.5 %collective-permute-start.73 = (bf16[2,4096]{1,0:T(2,128)(2,1)S(1)}, bf16[2,4096]{1,0:T(2,128)(2,1)S(1)}, u32[]{:S(2)}, u32[]{:S(2)}) collective-permute-start(bf16[2,4096]{1,0:T(2,128)(2,1)S(1)} %attend.1), channel_id=1, source_target_pairs={{0,24},{2,26},{4,28},{6,30},{8,16},{10,18},{12,20},{14,22},{16,8},... | collective-permute-start | bytes 49160 | tf_op jit(solution)/shard_map/ppermute | solution.py:217
  130.2 12.2 %collective-permute-start.74 = (bf16[2,4096]{1,0:T(2,128)(2,1)S(1)}, bf16[2,4096]{1,0:T(2,128)(2,1)S(1)}, u32[]{:S(2)}, u32[]{:S(2)}) collective-permute-start(bf16[2,4096]{1,0:T(2,128)(2,1)S(1)} %attend.1), channel_id=1, source_target_pairs={{0,28},{2,30},{4,24},{6,26},{8,20},{10,22},{12,16},{14,18},{16,12}... | collective-permute-start | bytes 49160 | tf_op jit(solution)/shard_map/ppermute | solution.py:217
  142.3 1.4 collective-permute-start.75
  144.4 9.2 %copy-start.4 = (bf16[2,16,512]{2,1,0:T(8,128)(2,1)S(1)}, bf16[2,16,512]{2,1,0:T(8,128)(2,1)}, u32[]{:S(2)}) copy-start(bf16[2,16,512]{2,1,0:T(8,128)(2,1)} %param.75) | copy-start | bytes 98308
  147.5 5.9 %collective-permute-start.76 = (f32[32,512]{1,0:T(8,128)S(1)}, f32[32,512]{1,0:T(8,128)S(1)}, u32[]{:S(2)}, u32[]{:S(2)}) collective-permute-start(f32[32,512]{1,0:T(8,128)S(1)} %fusion.16), channel_id=1, source_target_pairs={{0,1},{1,0},{2,3},{3,2},{4,5},{5,4},{6,7},{7,6},{8,9},{9,8},{10,11... | collective-permute-start | bytes 196616 | tf_op jit(solution)/shard_map/ppermute | solution.py:217

commit v2 on v1

v2 whole, which is shorter than its diff:
```python
import functools
import math

import jax
import jax.numpy as jnp
from jax import lax
from jax.experimental import pallas as pl
from jax.experimental.pallas import tpu as pltpu
from jax.sharding import PartitionSpec as P

STEPS = 2
JOINS = 2
TOTAL = STEPS * JOINS

epsilon = 1e-05

ROUNDS = [(0, 0, 0, 0), (0, 1, 0, 0), (0, 0, 1, 0), (0, 0, 0, 1),
          (0, 1, 1, 0), (0, 1, 0, 1), (0, 0, 1, 1), (0, 1, 1, 1)]


def plan_kernel(join_ref, plan_ref):
    me = lax.axis_index("rows")
    rows = lax.axis_size("rows")
    source, target, slot = [], [], []
    for s in range(STEPS):
        for j in range(JOINS):
            source.append(join_ref[s, j, 0])
            target.append(join_ref[s, j, 1])
            slot.append(join_ref[s, j, 2])
    one, zero = jnp.int32(1), jnp.int32(0)

    busy = []
    for i in range(TOTAL):
        for sender in (source[i], source[i] ^ 1):
            hit = zero
            for j in range(TOTAL):
                if j != i:
                    hit = hit | jnp.where(sender == target[j], one, zero)
            busy.append(hit)
    same = {}
    for i in range(TOTAL):
        for j in range(i + 1, TOTAL):
            same[i, j] = jnp.where(source[i] == (source[j] ^ 1), one, zero)
    single = zero
    swap = [zero] * TOTAL
    choices = sorted(range(2 ** TOTAL), key=lambda m: (-bin(m).count("1"), m))
    for m in choices:
        bits = [(m >> i) & 1 for i in range(TOTAL)]
        bad = zero
        for i in range(TOTAL):
            bad = bad | busy[2 * i + bits[i]]
        for (i, j), value in same.items():
            if bits[i] != bits[j]:
                bad = bad | value
        good = bad == 0
        single = jnp.where(good, one, single)
        swap = [jnp.where(good, jnp.int32(b), w) for b, w in zip(bits, swap)]

    clash = {}
    for i in range(TOTAL):
        for j in range(i + 1, TOTAL):
            both = (source[i] == target[j]) | (source[j] == target[i])
            clash[i, j] = jnp.where(both, one, zero)
    best = [zero] * TOTAL
    double = zero
    for rounds in reversed(ROUNDS):
        bad = zero
        for (i, j), value in clash.items():
            if rounds[i] == rounds[j]:
                bad = bad | value
        good = bad == 0
        double = jnp.where(good, one, double)
        best = [jnp.where(good, jnp.int32(r), b) for r, b in zip(rounds, best)]

    def kind_of(s, t):
        key = s ^ t
        return jnp.where(key == 0, 1, 2 * key + jnp.where(s < t, 0, 1))

    only, branch = zero, [zero, zero]
    arrives, step, place = zero, jnp.int32(STEPS), zero
    for i in range(TOTAL):
        s, t = source[i], target[i]
        sender = s ^ swap[i]
        part = (me == sender) | (me == t)
        only = jnp.where(part, kind_of(sender, t) + swap[i] * (2 * rows - 1), only)
        part = (me == s) | (me == t)
        for r in range(2):
            branch[r] = jnp.where(part & (best[i] == r), kind_of(s, t), branch[r])
        here = me == t
        arrives = jnp.where(here, best[i] + 1, arrives)
        step = jnp.where(here, i // JOINS, step)
        place = jnp.where(here, slot[i], place)
    plan_ref[0] = only
    plan_ref[1] = branch[0]
    plan_ref[2] = branch[1]
    plan_ref[3] = step
    plan_ref[4] = place
    plan_ref[5] = jnp.where(single > 0, 0, jnp.where(double > 0, 1, 2))
    plan_ref[6] = arrives
    plan_ref[7] = zero


def make_plan(join_list):
    return pl.pallas_call(
        plan_kernel,
        out_shape=jax.ShapeDtypeStruct((8,), jnp.int32),
        in_specs=[pl.BlockSpec(memory_space=pltpu.SMEM)],
        out_specs=pl.BlockSpec(memory_space=pltpu.SMEM),
        name="plan",
    )(join_list)


def transfer(branch, rows, *tiles):
    branches = [lambda *blocks: jnp.zeros_like(blocks[0])]

    def keep(index):
        return lambda *blocks: blocks[index]

    def send(index, pairs):
        return lambda *blocks: lax.ppermute(blocks[index], "rows", pairs)

    for index in range(len(tiles)):
        branches.append(keep(index))
        for key in range(1, rows):
            for low in (True, False):
                pairs = [(i, i ^ key) for i in range(rows) if (i < (i ^ key)) == low]
                branches.append(send(index, pairs))
    return lax.switch(branch, branches, *tiles)


def move_tiles(plan, join_list, rows, own, other):
    me = lax.axis_index("rows")

    def once(own, other):
        return transfer(plan[0], rows, own, other)

    def twice(own, other):
        first = transfer(plan[1], rows, own)
        second = transfer(plan[2], rows, own)
        late = plan[6] == 2
        return jnp.where(plan[6] == 1, first, jnp.where(late, second, jnp.zeros_like(own)))

    def summed(own, other):
        result = jnp.zeros_like(own)
        for s in range(STEPS):
            for j in range(JOINS):
                given = jnp.where(me == join_list[s, j, 0], own, jnp.zeros_like(own))
                given = lax.psum(given, "rows")
                result = jnp.where(me == join_list[s, j, 1], given, result)
        return result

    return lax.switch(plan[5], [once, twice, summed], own, other)


def attend_kernel(group, head_size, plan_ref, counts_ref, gain_ref, sums_ref, kv_ref, new_ref, out_ref, kept_ref):
    kept_ref[...] = new_ref[...]
    slots = kv_ref.shape[2]
    raw = sums_ref[0]
    for k in range(1, sums_ref.shape[0]):
        raw = raw + sums_ref[k]
    raw = jnp.concatenate(
        [raw[:, g * head_size:(g + 1) * head_size] for g in range(group)], axis=0
    )
    queries = (
        raw
        * lax.rsqrt(jnp.mean(raw * raw, axis=-1, keepdims=True) + epsilon)
        * gain_ref[...].astype(jnp.float32)
    ).astype(jnp.bfloat16)
    row = lax.broadcasted_iota(jnp.int32, (group * STEPS, 1), 0)
    second = lax.rem(row, STEPS) == 1
    join_step, join_slot = plan_ref[3], plan_ref[4]
    one, zero = jnp.int32(1), jnp.int32(0)

    def scores_of(keys, shown):
        scores = lax.dot_general(
            queries, keys, (((1,), (1,)), ((), ())), preferred_element_type=jnp.float32
        ) * (1.0 / math.sqrt(head_size))
        usable = jnp.where(second, shown[1], shown[0]) > 0
        return jnp.where(usable, scores, -1e30)

    all_scores = []
    for i in range(slots):
        shown = [
            jnp.where(
                (i < counts_ref[s, 0]) & ((join_step > s) | (join_slot != i)), one, zero
            )
            for s in range(STEPS)
        ]
        all_scores.append(scores_of(kv_ref[0, 0, i, :, :head_size], shown))
    shown = [jnp.where(join_step <= s, one, zero) for s in range(STEPS)]
    all_scores.append(scores_of(new_ref[0, :, :head_size], shown))
    highest = all_scores[0].max(axis=-1, keepdims=True)
    for scores in all_scores[1:]:
        highest = jnp.maximum(highest, scores.max(axis=-1, keepdims=True))
    exponents = [jnp.exp(scores - highest) for scores in all_scores]
    total = exponents[0].sum(axis=-1, keepdims=True)
    for exponent in exponents[1:]:
        total = total + exponent.sum(axis=-1, keepdims=True)
    context = jnp.zeros((group * STEPS, head_size), jnp.float32)
    for i in range(slots + 1):
        probs = (exponents[i] / total).astype(jnp.bfloat16)
        values = new_ref[0, :, head_size:] if i == slots else kv_ref[0, 0, i, :, head_size:]
        context = context + jnp.dot(probs, values, preferred_element_type=jnp.float32)
    context = jnp.concatenate(
        [context[g * STEPS:(g + 1) * STEPS] for g in range(group)], axis=1
    )
    out_ref[...] = context.astype(jnp.bfloat16)


def attend(plan, counts, query_gain, sums, kv_cache, arrived):
    _, kv_here, slots, tile_len, width = kv_cache.shape
    head_size = width // 2
    chips, _, columns = sums.shape
    heads_here = columns // head_size
    group = heads_here // kv_here
    wide = group * head_size
    smem = pl.BlockSpec(memory_space=pltpu.SMEM)
    return pl.pallas_call(
        functools.partial(attend_kernel, group, head_size),
        grid=(kv_here,),
        out_shape=(
            jax.ShapeDtypeStruct((STEPS, heads_here * head_size), jnp.bfloat16),
            jax.ShapeDtypeStruct(arrived.shape, jnp.bfloat16),
        ),
        in_specs=[
            smem,
            smem,
            pl.BlockSpec((1, head_size), lambda h: (0, 0)),
            pl.BlockSpec((chips, STEPS, wide), lambda h: (0, 0, h)),
            pl.BlockSpec((1, 1, slots, tile_len, width), lambda h: (0, h, 0, 0, 0)),
            pl.BlockSpec((1, tile_len, width), lambda h: (h, 0, 0)),
        ],
        out_specs=(
            pl.BlockSpec((STEPS, wide), lambda h: (0, h)),
            pl.BlockSpec((1, tile_len, width), lambda h: (h, 0, 0)),
        ),
        compiler_params=pltpu.CompilerParams(vmem_limit_bytes=53 * 1024 * 1024),
        cost_estimate=pl.CostEstimate(
            flops=4 * kv_here * (slots + 1) * tile_len * width * group,
            bytes_accessed=kv_here * (slots + 1) * tile_len * width * 2,
            transcendentals=kv_here * (slots + 1) * tile_len * group * STEPS,
        ),
        name="attend",
    )(plan, counts, query_gain.reshape(1, head_size), sums, kv_cache, arrived)


def on_device(
    rows,
    heads,
    hidden,
    norm_gain,
    query_weight,
    query_gain,
    out_weight,
    attn_gate,
    kv_cache,
    new_tiles,
    counts,
    join_list,
):
    width = hidden.shape[2]
    me = lax.axis_index("rows")
    odd = (me & 1) > 0
    chips = rows // 2
    own_tile = new_tiles[0]
    plan = make_plan(join_list)

    def across(block, axis, size, key):
        return lax.ppermute(block, axis, [(i, i ^ key) for i in range(size)])

    same_core = [list(range(core, rows, 2)) for core in range(2)]

    def between_chips(blocks):
        return lax.all_to_all(blocks, "rows", 0, 0, axis_index_groups=same_core, tiled=True)

    other_tile = across(own_tile, "rows", rows, 1)
    wide_hidden = hidden.astype(jnp.float32)
    scaled = (wide_hidden * norm_gain.astype(jnp.float32)).astype(jnp.bfloat16)
    scaled = scaled.reshape(STEPS, chips, 2, width).transpose(2, 1, 0, 3)
    scaled = jnp.where(odd, scaled[::-1], scaled)
    partial = jnp.dot(
        scaled.reshape(rows * STEPS, width), query_weight, preferred_element_type=jnp.float32
    )
    columns = partial.shape[1]
    partial = partial.reshape(2, chips, STEPS, columns)
    sums = between_chips(partial[0] + across(partial[1], "rows", rows, 1))
    arrived = move_tiles(plan, join_list, rows, own_tile, other_tile)
    context, arrived = attend(plan, counts, query_gain, sums, kv_cache, arrived)
    mine = between_chips(jnp.broadcast_to(context, (chips, STEPS, columns)))
    theirs = across(mine, "rows", rows, 1)
    gathered = jnp.stack(
        [jnp.where(odd, theirs, mine), jnp.where(odd, mine, theirs)], axis=1
    )
    gathered = gathered.transpose(2, 0, 1, 3).reshape(STEPS * rows, columns)
    projected = jnp.dot(gathered, out_weight, preferred_element_type=jnp.float32)
    key = 1
    while key < heads:
        projected = projected + across(projected, "heads", heads, key)
        key *= 2
    projected = projected.reshape(STEPS, rows, width)
    mixed = (wide_hidden + jnp.tanh(attn_gate[0]) * projected).astype(jnp.bfloat16)
    return mixed, arrived[None]


def solution(mesh):
    in_specs = (
        P(None, None, "rows"),
        P("rows"),
        P("rows", "heads"),
        P(),
        P("heads", "rows"),
        P(),
        P("rows", "heads", None, None, None),
        P("rows", "heads", None, None),
        P(None, "rows"),
        P(),
    )
    out_specs = (P(None, None, "rows"), P("rows", "heads", None, None))
    body = functools.partial(on_device, mesh.shape["rows"], mesh.shape["heads"])
    return jax.shard_map(
        body, mesh=mesh, in_specs=in_specs, out_specs=out_specs, check_vma=False
    )
```

time: 163 us -> 102 us (0.63)
  starting transfers between devices: 101 us -> 10.4 us
  waiting for transfers between devices: 17.2 us -> 41.3 us
  blocking collectives: 0 us -> 10.5 us
  local copies, waits for them, and re-layouts: 6.92 us -> 2.34 us
  between operations: 18.2 us -> 15.5 us
  other arithmetic: 2.37 us -> 4.21 us
  Pallas kernels: 8.86 us -> 10.5 us
    ppermute x17 -> x4, starting transfers between devices: 101 us -> 2.18 us  [across(): return lax.ppermute(block, axis, [(i, i ^ key) for i in range(size)])]
    ppermute x0 -> x1, waiting for transfers between devices: none -> 36.2 us  [send(): return lambda *blocks: lax.ppermute(blocks[index], 'rows', pairs)]
    ppermute x17 -> x4, waiting for transfers between devices: 17.2 us -> 5.06 us  [across(): return lax.ppermute(block, axis, [(i, i ^ key) for i in range(size)])]
    all_to_all x0 -> x1, blocking collectives: none -> 10.5 us  [between_chips(): lax.all_to_all(blocks, 'rows', 0, 0, axis_index_groups=same_core, tiled=T...]
    all_to_all x0 -> x1, starting transfers between devices: none -> 6.95 us  [between_chips(): lax.all_to_all(blocks, 'rows', 0, 0, axis_index_groups=same_core, tiled=T...]
    another operation x5 -> x0, local copies, waits for them, and re-layouts: 3.76 us -> none
    add x2 -> x1, other arithmetic: 0.28 us -> 1.92 us  [on_device(): sums = between_chips(partial[0] + across(partial[1], 'rows', rows, 1))]
  transfers between devices with their start and end apart: 17 -> 6, of which waited for: 5 -> 4; matrix products, arithmetic and copies ran while one was open for 3% -> 8% of each run, Pallas kernels for 1% -> 1%
where the time goes in v2:
time: 102 us; the launch traced here: 101 us
  waiting for transfers between devices  41.3 us (40%)
  between operations  15.5 us (15%)
  Pallas kernels  10.5 us (10%)
  blocking collectives  10.5 us (10%)
  starting transfers between devices  10.4 us (10%)
  matrix products  6.01 us (6%)
  other arithmetic  4.21 us (4%)
  local copies, waits for them, and re-layouts  2.34 us (2%)
    ppermute x1, waiting for transfers between devices, send(): return lambda *blocks: lax.ppermute(blocks[index], 'rows', pairs)  36.2 us
    all_to_all x1, blocking collectives, between_chips(): lax.all_to_all(blocks, 'rows', 0, 0, axis_index_groups=same_core, tiled=T...  10.5 us
    pallas_call x1, Pallas kernels, attend(): pl.pallas_call(functools.partial(attend_kernel, group, head_size), grid=(...  9.15 us
    all_to_all x1, starting transfers between devices, between_chips(): lax.all_to_all(blocks, 'rows', 0, 0, axis_index_groups=same_core, tiled=T...  6.95 us
    ppermute x4, waiting for transfers between devices, across(): return lax.ppermute(block, axis, [(i, i ^ key) for i in range(size)])  5.06 us
    dot_general x1, matrix products, on_device(): jnp.dot(scaled.reshape(rows * STEPS, width), query_weight, preferred_elem...  3.01 us
    dot_general x1, matrix products, on_device(): jnp.dot(gathered, out_weight, preferred_element_type=jnp.float32)  2.99 us
    ppermute x4, starting transfers between devices, across(): return lax.ppermute(block, axis, [(i, i ^ key) for i in range(size)])  2.18 us
  transfers between devices with their start and end apart: 6, of which 4 were waited for; matrix products, arithmetic and copies ran while one was open for 8% of the time, Pallas kernels for 1%

profile of v2, /device:TPU:0, one launch (start us, length us, event | category | flops | bytes accessed | tf_op | source)
XLA Modules:
  0.0 100.9 jit_solution(50320552822889017)
XLA Ops:
  7.2 0.5 collective-permute-start.121
  7.7 0.7 convert_element_type.13
  8.4 0.8 fusion
  9.3 3.0 %fusion.5 = f32[32,4096]{1,0:T(8,128)S(1)} fusion(bf16[32,512]{1,0:T(8,128)(2,1)S(1)} %reshape.44, bf16[512,4096]{1,0:T(8,128)(2,1)} %param.142), kind=kOutput, calls=%fused_computation.19 | convolution fusion | flops 134217728 | bytes 4751360 | tf_op jit(solution)/shard_map/dot_general | solution.py:281
  12.3 0.9 squeeze.320
  13.3 0.2 squeeze.319
  13.4 1.7 %collective-permute-done.120 = f32[8,2,4096]{2,1,0:T(2,128)} collective-permute-done((f32[8,2,4096]{2,1,0:T(2,128)}, f32[8,2,4096]{2,1,0:T(2,128)}, u32[]{:S(2)}, u32[]{:S(2)}) %collective-permute-start.120) | collective-permute-done | bytes 262176 | tf_op jit(solution)/shard_map/ppermute | solution.py:269
  15.1 1.9 %add.17 = f32[8,2,4096]{2,1,0:T(2,128)} add(f32[8,2,4096]{2,1,0:T(2,128)S(1)} %squeeze.319, f32[8,2,4096]{2,1,0:T(2,128)} %collective-permute-done.120) | non-fusion elementwise | flops 65536 | bytes 786432 | tf_op jit(solution)/shard_map/add | solution.py:286
  17.0 7.0 %all-to-all-start = ((f32[8,2,4096]{2,1,0:T(2,128)}), f32[8,2,4096]{2,1,0:T(2,128)S(1)}, u32[]{:S(2)}, u32[]{:S(2)}) async-start(f32[8,2,4096]{2,1,0:T(2,128)} %add.17), calls=%async_computation | async-start | bytes 524288 | tf_op jit(solution)/shard_map/all_to_all | solution.py:274
  24.0 1.3 %plan.1.plan_ref = s32[8]{0:T(128)S(1)} custom-call(s32[2,2,3]{2,1,0:T(2,128)S(1)} %copy-done.3), custom_call_target="tpu_custom_call" | custom-call | tf_op jit(solution)/shard_map/plan/pallas_call | solution.py:104
  25.3 0.6 slice.50
  26.7 37.6 %conditional.4 = (bf16[4,1408,256]{2,1,0:T(8,128)(2,1)}) conditional(s32[]{:T(128)} %bitcast.16, (s32[8]{0:T(128)S(1)}, bf16[4,1408,256]{2,1,0:T(8,128)(2,1)S(1)}, bf16[4,1408,256]{2,1,0:T(8,128)(2,1)}) %tuple.549, (s32[8]{0:T(128)S(1)}, bf16[4,1408,256]{2,1,0:T(8,128)(2,1)S(1)}) %tuple.550, (s32[2,2,3]{2,1,0:T(2,128)S(1)}, ...), branch_computations={%region_0.64_spmd, %region_64.129_spmd, %region_129.134_spmd} | conditional | flops 17301512 | bytes 98042040 | solution.py:152
  26.7 37.5 %conditional = (bf16[4,1408,256]{2,1,0:T(8,128)(2,1)}) conditional(s32[]{:T(128)} %bitcast, () %tuple.390, bf16[4,1408,256]{2,1,0:T(8,128)(2,1)S(1)} %get-tuple-element.271, bf16[4,1408,256]{2,1,0:T(8,128)(2,1)S(1)} %get-tuple-element.271, bf16[4,1408,256]{2,1,0:T(8,128)(2,1)S(1)} %get-tuple-element.271, ...), branch_computations={%region_1.1_spmd, %region_2.2_spmd, %region_3.3_spmd, %region_4.4_... | conditional | bytes 11534384 | solution.py:128
  26.7 1.3 %collective-permute-start.13 = (bf16[4,1408,256]{2,1,0:T(8,128)(2,1)S(1)}, bf16[4,1408,256]{2,1,0:T(8,128)(2,1)}, u32[]{:S(2)}, u32[]{:S(2)}) collective-permute-start(bf16[4,1408,256]{2,1,0:T(8,128)(2,1)S(1)} %param.15), channel_id=1, source_target_pairs={{8,6},{10,4},{12,2},{14,0},{24,22},{26,20},{28,18},{30,16},{9,7},{... | collective-permute-start | bytes 8650760 | tf_op jit(solution)/shard_map/cond/branch_0_fun/cond/branch_15_fun/ppermute | solution.py:120
  28.0 36.2 %collective-permute-done.13 = bf16[4,1408,256]{2,1,0:T(8,128)(2,1)} collective-permute-done((bf16[4,1408,256]{2,1,0:T(8,128)(2,1)S(1)}, bf16[4,1408,256]{2,1,0:T(8,128)(2,1)}, u32[]{:S(2)}, u32[]{:S(2)}) %collective-permute-start.13) | collective-permute-done | bytes 2883616 | tf_op jit(solution)/shard_map/cond/branch_0_fun/cond/branch_15_fun/ppermute | solution.py:120
  64.3 9.1 %attend.1 = (bf16[2,4096]{1,0:T(2,128)(2,1)S(1)}, bf16[4,1408,256]{2,1,0:T(8,128)(2,1)}) custom-call(s32[8]{0:T(128)S(1)} %plan.1.plan_ref, s32[2,1]{1,0:T(2,128)S(1)} %copy.20.counts_ref, bf16[1,128]{1,0:T(2,128)(2,1)S(1)} %bitcast.33, f32[8,2,4096]{2,1,0:T(2,128)S(1)} %all-to-all-done.sums_ref, bf16[1,4,4,1408,256]{4,3,2,1,0:T(8,128)(2,1)} %kv_ref.1, ...), custom_call_target="tpu_custom_call" | custom-call | flops 230686720 | bytes 14417920 | tf_op jit(solution)/shard_map/attend/pallas_call | solution.py:218
  73.5 10.5 %all_to_all.10 = bf16[8,2,4096]{2,1,0:T(2,128)(2,1)S(1)} all-to-all(bf16[8,2,4096]{2,1,0:T(2,128)(2,1)S(1)} %broadcast_in_dim.7), channel_id=1, replica_groups={{0,4,8,12,16,20,24,28},{2,6,10,14,18,22,26,30},{1,5,9,13,17,21,25,29},{..., dimensions={0} | all-to-all | bytes 262144 | tf_op jit(solution)/shard_map/all_to_all | solution.py:274
  84.2 1.3 %collective-permute-done.122 = bf16[8,2,4096]{2,0,1:T(8,128)(2,1)S(1)} collective-permute-done((bf16[8,2,4096]{2,0,1:T(8,128)(2,1)S(1)}, bf16[8,2,4096]{2,0,1:T(8,128)(2,1)S(1)}, u32[]{:S(2)}, u32[]{:S(2)}) %collective-permute-start.122) | collective-permute-done | bytes 131104 | tf_op jit(solution)/shard_map/ppermute | solution.py:269
  85.5 0.2 select_bitcast_fusion.1
  85.7 0.3 copy.24
  86.1 3.0 %fusion.6 = f32[32,512]{1,0:T(8,128)S(1)} fusion(bf16[32,4096]{1,0:T(8,128)(2,1)S(1)} %reshape.45, bf16[4096,512]{1,0:T(8,128)(2,1)} %param.144), kind=kOutput, calls=%fused_computation.20 | convolution fusion | flops 134217728 | bytes 4521984 | tf_op jit(solution)/shard_map/dot_general | solution.py:295
  89.1 1.5 %collective-permute-start.123 = (f32[32,512]{1,0:T(8,128)S(1)}, f32[32,512]{1,0:T(8,128)S(1)}, u32[]{:S(2)}, u32[]{:S(2)}) collective-permute-start(f32[32,512]{1,0:T(8,128)S(1)} %fusion.6), channel_id=1, source_target_pairs={{0,1},{1,0},{2,3},{3,2},{4,5},{5,4},{6,7},{7,6},{8,9},{9,8},{10,11... | collective-permute-start | bytes 196616 | tf_op jit(solution)/shard_map/ppermute | solution.py:269
  91.3 2.1 %collective-permute-done.123 = f32[32,512]{1,0:T(8,128)S(1)} collective-permute-done((f32[32,512]{1,0:T(8,128)S(1)}, f32[32,512]{1,0:T(8,128)S(1)}, u32[]{:S(2)}, u32[]{:S(2)}) %collective-permute-start.123) | collective-permute-done | bytes 65568 | tf_op jit(solution)/shard_map/ppermute | solution.py:269
  93.4 0.6 fusion.1
  (25 shorter events, 0.7 us)
Async XLA Ops:
  7.2 19.5 %collective-permute-start.121 = (bf16[4,1408,256]{2,1,0:T(8,128)(2,1)}, bf16[4,1408,256]{2,1,0:T(8,128)(2,1)}, u32[]{:S(2)}, u32[]{:S(2)}) collective-permute-start(bf16[4,1408,256]{2,1,0:T(8,128)(2,1)} %bitcast.34), channel_id=1, source_target_pairs={{0,2},{2,0},{4,6},{6,4},{8,10},{10,8},{12,14},{14,12},{16,18},{18,... | collective-permute-start | bytes 8650760 | tf_op jit(solution)/shard_map/ppermute | solution.py:269
  12.3 11.7 %copy-start.3 = (s32[2,2,3]{2,1,0:T(2,128)S(1)}, s32[2,2,3]{2,1,0:T(2,128)}, u32[]{:S(2)}) copy-start(s32[2,2,3]{2,1,0:T(2,128)} %join_ref.1) | copy-start | bytes 148
  12.3 13.6 %copy-start.4 = (s32[2,1]{0,1:T(1,128)S(1)}, s32[2,1]{0,1:T(1,128)}, u32[]{:S(2)}) copy-start(s32[2,1]{0,1:T(1,128)} %param.148) | copy-start | bytes 28
  12.3 14.3 %copy-start.1 = (bf16[1,4,1408,256]{3,2,1,0:T(8,128)(2,1)S(1)}, bf16[1,4,1408,256]{3,2,1,0:T(8,128)(2,1)}, u32[]{:S(2)}) copy-start(bf16[1,4,1408,256]{3,2,1,0:T(8,128)(2,1)} %param.147) | copy-start | bytes 8650756
  13.2 1.9 %collective-permute-start.120 = (f32[8,2,4096]{2,1,0:T(2,128)}, f32[8,2,4096]{2,1,0:T(2,128)}, u32[]{:S(2)}, u32[]{:S(2)}) collective-permute-start(f32[8,2,4096]{2,1,0:T(2,128)} %squeeze.320), channel_id=1, source_target_pairs={{0,2},{2,0},{4,6},{6,4},{8,10},{10,8},{12,14},{14,12},{16,18},{18,... | collective-permute-start | bytes 786440 | tf_op jit(solution)/shard_map/ppermute | solution.py:269
  17.0 47.3 %all-to-all-start = ((f32[8,2,4096]{2,1,0:T(2,128)}), f32[8,2,4096]{2,1,0:T(2,128)S(1)}, u32[]{:S(2)}, u32[]{:S(2)}) async-start(f32[8,2,4096]{2,1,0:T(2,128)} %add.17), calls=%async_computation | async-start | bytes 524288 | tf_op jit(solution)/shard_map/all_to_all | solution.py:274
  26.6 37.6 %copy-start = (bf16[128]{0:T(256)(128)(2,1)S(1)}, bf16[128]{0:T(256)(128)(2,1)}, u32[]{:S(2)}) copy-start(bf16[128]{0:T(256)(128)(2,1)} %param.143) | copy-start | bytes 772
  26.7 37.5 %collective-permute-start.13 = (bf16[4,1408,256]{2,1,0:T(8,128)(2,1)S(1)}, bf16[4,1408,256]{2,1,0:T(8,128)(2,1)}, u32[]{:S(2)}, u32[]{:S(2)}) collective-permute-start(bf16[4,1408,256]{2,1,0:T(8,128)(2,1)S(1)} %param.15), channel_id=1, source_target_pairs={{8,6},{10,4},{12,2},{14,0},{24,22},{26,20},{28,18},{30,16},{9,7},{... | collective-permute-start | bytes 8650760 | tf_op jit(solution)/shard_map/cond/branch_0_fun/cond/branch_15_fun/ppermute | solution.py:120
  84.1 1.4 %collective-permute-start.122 = (bf16[8,2,4096]{2,0,1:T(8,128)(2,1)S(1)}, bf16[8,2,4096]{2,0,1:T(8,128)(2,1)S(1)}, u32[]{:S(2)}, u32[]{:S(2)}) collective-permute-start(bf16[8,2,4096]{2,0,1:T(8,128)(2,1)S(1)} %copy.21), channel_id=1, source_target_pairs={{0,2},{2,0},{4,6},{6,4},{8,10},{10,8},{12,14},{14,12},{16,18},{18,... | collective-permute-start | bytes 393224 | tf_op jit(solution)/shard_map/ppermute | solution.py:269
  85.7 7.7 %copy-start.2 = (bf16[2,16,512]{2,1,0:T(8,128)(2,1)S(1)}, bf16[2,16,512]{2,1,0:T(8,128)(2,1)}, u32[]{:S(2)}) copy-start(bf16[2,16,512]{2,1,0:T(8,128)(2,1)} %param.140) | copy-start | bytes 98308
  89.1 4.3 %collective-permute-start.123 = (f32[32,512]{1,0:T(8,128)S(1)}, f32[32,512]{1,0:T(8,128)S(1)}, u32[]{:S(2)}, u32[]{:S(2)}) collective-permute-start(f32[32,512]{1,0:T(8,128)S(1)} %fusion.6), channel_id=1, source_target_pairs={{0,1},{1,0},{2,3},{3,2},{4,5},{5,4},{6,7},{7,6},{8,9},{9,8},{10,11... | collective-permute-start | bytes 196616 | tf_op jit(solution)/shard_map/ppermute | solution.py:269
